TPU v7x, 32 devices: a whole 2x2x4 slice. The times are simulated.
32 devices in a mesh: groups: 2 (over y), pairs: 4 (over z), sub: 2 (over x), rep: 2 (over core).
Axes of the slice: x: 2, y: 2, z: 4, core: 2. Of those that a mesh axis runs over, the one named last changes fastest.
Arguments:
- amplitudes: float32 [32, 256, 256], P(('groups', 'pairs', 'sub')), parts along dimension 0, may hold values from -6 to 6
- exchange_ints: float32 [32, 256, 256], P(('groups', 'pairs', 'sub')), parts along dimension 0, may hold values from -6 to 6
- pair_list: int32 [32, 2], P(('groups', 'pairs', 'sub')), parts along dimension 0, may hold values from 0 to 1999
- domains: int32 [32, 256], P(('groups', 'pairs', 'sub')), parts along dimension 0, may hold values from 0 to 23999, as said below
- link_source: int32 [32, 32], P(('groups', 'pairs', 'sub')), parts along dimension 0, may hold values from 0 to 15, as said below
- link_entry: int32 [32, 32], P(('groups', 'pairs', 'sub')), parts along dimension 0, may hold values from 0 to 4095
- link_count: int32 [32], P(('groups', 'pairs', 'sub')), parts along dimension 0, may hold values from 16 to 32, as said below
- owner_map: int32 [32], P('groups'), parts along dimension 0, may hold values from 0 to 15, as said below
- fock_values: float32 [8192], P('groups'), parts along dimension 0, may hold values from -0.6 to 0.6
- occ_energy: float32 [4000], P('groups'), parts along dimension 0, may hold values from -1.5 to -0.3
- vir_energy: float32 [48000], P('groups'), parts along dimension 0, may hold values from 0.2 to 3
- positions: float32 [3, 48000], P(None, 'groups'), parts along dimension 1
Outputs:
- residual: float32 [32, 256, 256], P(('groups', 'pairs', 'sub')), parts along dimension 0
- updated: float32 [32, 256, 256], P(('groups', 'pairs', 'sub')), parts along dimension 0
There are 2 independent parts, one for each index of `groups`. A program takes and returns all parts, laid end to end along the dimension named above; each array names one. Nothing has to cross between parts.
Inputs may be any that keep to these rules, and one draw needn't show every extreme that they name: `domains`: each row names 256 distinct orbitals. `link_source`: pair ids. Over the live slots of the pairs stored on one device, the named neighbours lie on at most one distinct storage slot of each index of pairs, always on a device with the same index of sub; every device names one on each of min(4, live slots) indices. `link_count`: every fifth stored pair has all 32 slots live. `owner_map`: A permutation.
All inputs are finite; a program needn't handle non-finite values.
Results may differ from a plain program's by a relative error of at most 0.0003.
Values sent between devices are 32-bit elements; how exact they have to be, the bound alone decides.
No kernel may reach another device: no remote copies, remote signals or barrier semaphores. Data moves between devices by JAX's collectives and lax.ppermute only.
A program may use at most 64 MiB of HBM per device.

v0:
```python
import functools

import jax
import jax.numpy as jnp
from jax import lax
from jax.experimental import pallas as pl
from jax.experimental.pallas import tpu as pltpu
from jax.sharding import PartitionSpec as P

intersection_rate = 2.0
COORD_ROWS = 8
LOG2_E = 1.4426950408889634
VMEM_LIMIT = 40 * 1024 * 1024


def product(left, right):
    return jnp.dot(left, right, precision=lax.Precision.HIGHEST, preferred_element_type=jnp.float32)


def pick_row(array, index):
    return lax.dynamic_index_in_dim(array, index, 0, keepdims=False)


def model_intersection(left_coords, right_coords):
    squared = jnp.zeros((left_coords.shape[1], right_coords.shape[1]), jnp.float32)
    for component in range(3):
        gap_now = left_coords[component][:, None] - right_coords[component][None, :]
        squared = squared + gap_now * gap_now
    return jnp.exp(-intersection_rate * squared)


def pair_local(block, integrals, pair_coords, pair_energy, pair_shift):
    metric = model_intersection(pair_coords, pair_coords)
    virtual_fock = metric * ((pair_energy[:, None] + pair_energy[None, :]) * 0.5)
    right_side = product(block, metric)
    left_side = product(metric, block)
    return (
        integrals
        + product(virtual_fock, right_side)
        + product(left_side, virtual_fock)
        - pair_shift * product(metric, right_side)
    )


def on_device_any(
    amplitudes,
    exchange_ints,
    pair_list,
    domains,
    link_source,
    link_entry,
    link_count,
    owner_map,
    fock_values,
    occ_energy,
    vir_energy,
    positions,
):
    pair_count = amplitudes.shape[0]
    link_slots = link_source.shape[1]
    row_count = lax.axis_size("pairs")
    sub_count = lax.axis_size("sub")
    core_count = lax.axis_size("rep")
    my_core = lax.axis_index("rep")
    coords = jnp.moveaxis(jnp.take(positions, domains, axis=1), 0, 1)
    energy = jnp.take(vir_energy, domains, axis=0)
    shift = jnp.take(occ_energy, pair_list[:, 0]) + jnp.take(occ_energy, pair_list[:, 1])
    is_live = jnp.arange(link_slots, dtype=jnp.int32)[None, :] < link_count[:, None]
    source_loc = jnp.take(owner_map, link_source)
    source_peer = source_loc // (pair_count * sub_count)
    source_slot = source_loc % pair_count
    peers = jnp.arange(row_count, dtype=jnp.int32)
    matched = is_live[:, :, None] & (source_peer[:, :, None] == peers[None, None, :])
    fock_weight = jnp.take(fock_values, link_entry)
    weight = jnp.sum(jnp.where(matched, fock_weight[:, :, None], 0.0), axis=1)
    wanted = jnp.max(jnp.where(matched, source_slot[:, :, None], 0), axis=(0, 1))
    asked = lax.all_to_all(wanted[:, None], "pairs", split_axis=0, concat_axis=0, tiled=True)[:, 0]
    fetched = lax.all_to_all(
        jnp.take(amplitudes, asked, axis=0), "pairs", split_axis=0, concat_axis=0, tiled=True
    )
    fetched_coords = lax.all_to_all(
        jnp.take(coords, asked, axis=0), "pairs", split_axis=0, concat_axis=0, tiled=True
    )

    def target(pair):
        local = pair_local(
            pick_row(amplitudes, pair),
            pick_row(exchange_ints, pair),
            pick_row(coords, pair),
            pick_row(energy, pair),
            pick_row(shift, pair),
        )

        def advance(peer, total):
            intersection = model_intersection(pick_row(coords, pair), pick_row(fetched_coords, peer))
            term = product(product(intersection, pick_row(fetched, peer)), intersection.T)
            return total - pick_row(pick_row(weight, pair), peer) * term

        return lax.fori_loop(0, row_count, advance, local)

    mine = jnp.arange(pair_count, dtype=jnp.int32) % core_count == my_core
    share = lax.map(
        lambda pair: lax.cond(
            pick_row(mine, pair), target, lambda _: jnp.zeros_like(amplitudes[0]), pair
        ),
        jnp.arange(pair_count, dtype=jnp.int32),
    )
    residual = lax.psum(share, "rep")
    denominator = energy[:, :, None] + energy[:, None, :] - shift[:, None, None]
    return residual, amplitudes - residual / denominator


def split(value):
    high = value.astype(jnp.bfloat16)
    low = (value - high.astype(jnp.float32)).astype(jnp.bfloat16)
    return high, low


NN = (((1,), (0,)), ((), ()))
NT = (((1,), (1,)), ((), ()))
TN = (((0,), (0,)), ((), ()))


def dot(left, right, dims):
    return lax.dot_general(left, right, dims, preferred_element_type=jnp.float32)


def dot3(left, right, dims=NN):
    return (
        dot(left[0], right[0], dims) + dot(left[0], right[1], dims) + dot(left[1], right[0], dims)
    )


def overlap(column, rows):
    squared = None
    for c in range(3):
        gap = column[:, c : c + 1] - rows[c : c + 1, :]
        squared = gap * gap if squared is None else squared + gap * gap
    return jnp.exp2(-intersection_rate * LOG2_E * squared)


def overlap_spread(spread_ref, p, rows):
    halves = []
    for k in range(rows.shape[1] // 128):
        squared = None
        for c in range(3):
            gap = spread_ref[p, c] - rows[c : c + 1, k * 128 : (k + 1) * 128]
            squared = gap * gap if squared is None else squared + gap * gap
        halves.append(jnp.exp2(-intersection_rate * LOG2_E * squared))
    return halves


def sandwich(metric, block):
    metric = split(metric)
    return dot3(split(dot3(metric, split(block))), metric, NT)


def start_all(copies):
    for copy in copies:
        copy.start()
    return copies


def parts_of(value, divisor):
    if divisor & (divisor - 1) == 0:
        return value >> (divisor.bit_length() - 1), value & (divisor - 1)
    return lax.div(value, divisor), lax.rem(value, divisor)


def partners():
    row = lax.axis_index("pairs")
    return row ^ (3 - lax.axis_index("rep")), row ^ 1


def open_kernel(
    sub_count,
    source_hbm,
    count_hbm,
    owner_hbm,
    domains_hbm,
    block_hbm,
    message_ref,
    wanted_near_ref,
    halves_ref,
    source_ref,
    count_ref,
    owner_ref,
    domains_ref,
    sems,
):
    pairs, links = source_ref.shape
    size = domains_ref.shape[1]
    half = size // 2
    start = pl.multiple_of(lax.axis_index("rep") * half, half)
    moves = [
        (source_hbm, source_ref),
        (count_hbm, count_ref),
        (owner_hbm, owner_ref),
        (domains_hbm, domains_ref),
    ]
    moves += [
        (block_hbm.at[p, pl.ds(start, half), :], halves_ref.at[p, pl.ds(0, half), :])
        for p in range(pairs)
    ]
    copies = [
        pltpu.make_async_copy(source, target, sems.at[k])
        for k, (source, target) in enumerate(moves)
    ]
    for copy in copies:
        copy.start()
    for copy in copies[:4]:
        copy.wait()
    source = source_ref[...]
    pair = lax.broadcasted_iota(jnp.int32, (pairs, links), 0)
    limit = jnp.zeros_like(source)
    for p in range(pairs):
        limit = jnp.where(pair == p, count_ref[p], limit)
    live = lax.broadcasted_iota(jnp.int32, (pairs, links), 1) < limit
    place = jnp.zeros_like(source)
    for k in range(owner_ref.shape[0]):
        place = jnp.where(source == k, owner_ref[k], place)
    there, _ = parts_of(place, pairs * sub_count)
    _, slot = parts_of(place, pairs)
    for peer, wanted_ref in zip(partners(), (message_ref, wanted_near_ref)):
        wish = jnp.where(live & (there == peer), slot, 0)
        wanted_ref[...] = jnp.broadcast_to(jnp.max(wish, keepdims=True), (8, 128))
    for p in range(pairs):
        for k in range(2):
            row = 4 + 2 * p + k
            message_ref[row : row + 1, :] = domains_ref[p : p + 1, k * 128 : (k + 1) * 128]
        halves_ref[p, half:, :] = jnp.broadcast_to(
            domains_ref[p : p + 1, :].astype(jnp.float32), (COORD_ROWS, size)
        )
    for copy in copies[4:]:
        copy.wait()


def look_up(index, table_ref, components, held):
    count = index.shape[1]
    rows = table_ref.shape[0] // held
    table = table_ref[: components * rows, :]
    first = table.astype(jnp.bfloat16)
    left = table - first.astype(jnp.float32)
    second = left.astype(jnp.bfloat16)
    third = (left - second.astype(jnp.float32)).astype(jnp.bfloat16)
    high = index // 128
    low = index - high * 128
    chosen = (lax.broadcasted_iota(jnp.int32, (rows, count), 0) == high).astype(
        jnp.float32
    ).astype(jnp.bfloat16)
    lane = lax.broadcasted_iota(jnp.int32, (128, count), 0) == low
    found = []
    for c in range(components):
        span = slice(c * rows, (c + 1) * rows)
        lines = (
            dot(first[span], chosen, TN)
            + dot(second[span], chosen, TN)
            + dot(third[span], chosen, TN)
        )
        found.append(jnp.sum(jnp.where(lane, lines, 0.0), axis=0, keepdims=True))
    return found


def domain_of(message_ref, p):
    row = 4 + 2 * p
    return jnp.concatenate([message_ref[row : row + 1, :], message_ref[row + 1 : row + 2, :]], axis=1)


def centres_kernel(
    positions_hbm,
    energy_hbm,
    message_ref,
    asked_ref,
    coords_ref,
    far_ref,
    table,
    positions_ref,
    energy_ref,
    sems,
):
    copies = [
        pltpu.make_async_copy(positions_hbm, positions_ref, sems.at[0]),
        pltpu.make_async_copy(energy_hbm, energy_ref, sems.at[1]),
    ]
    for copy in copies:
        copy.start()
    pairs, size = coords_ref.shape[0], coords_ref.shape[2]
    orbitals = positions_ref.shape[1]
    rows = table.shape[0] // 4
    whole, rest = orbitals // 128, orbitals % 128
    for c in range(4):
        table[c * rows + whole : (c + 1) * rows, :] = jnp.zeros((rows - whole, 128), jnp.float32)
    for copy in copies:
        copy.wait()
    for k in range(whole):
        table[pl.ds(k, 3, stride=rows), :] = positions_ref[:, k * 128 : (k + 1) * 128]
        table[3 * rows + k : 3 * rows + k + 1, :] = energy_ref[k * 128 : (k + 1) * 128].reshape(1, 128)
    if rest:
        table[pl.ds(whole, 3, stride=rows), :rest] = positions_ref[:, whole * 128 :]
        table[3 * rows + whole : 3 * rows + whole + 1, :rest] = energy_ref[whole * 128 :].reshape(
            1, rest
        )
    slot_one = jnp.max(message_ref[0:1, :]) > 0
    index = [domain_of(message_ref, p) for p in range(pairs)]
    index.append(jnp.where(slot_one, domain_of(asked_ref, 1), domain_of(asked_ref, 0)))
    found = look_up(jnp.concatenate(index, axis=1), table, 4, 4)
    found.append(jnp.zeros((COORD_ROWS - 4, (pairs + 1) * size), jnp.float32))
    found = jnp.concatenate(found, axis=0)
    for p in range(pairs):
        coords_ref[p] = found[:, p * size : (p + 1) * size]
    far_ref[...] = found[:, pairs * size :]


def select_kernel(asked_ref, block_ref, payload_ref):
    for k in range(payload_ref.shape[1] // 128):
        span = slice(k * 128, (k + 1) * 128)
        slot_one = jnp.broadcast_to(asked_ref[0:1, :], (payload_ref.shape[0], 128)) > 0
        payload_ref[:, span] = jnp.where(slot_one, block_ref[1, :, span], block_ref[0, :, span])


def own_kernel(
    sub_count,
    block_ref,
    integrals_ref,
    coords_ref,
    far_rows_ref,
    source_hbm,
    entry_hbm,
    count_hbm,
    owner_hbm,
    fock_hbm,
    pair_hbm,
    occ_hbm,
    share_ref,
    weight_ref,
    inverse_ref,
    spread_ref,
    high_ref,
    low_ref,
    source_ref,
    entry_ref,
    count_ref,
    owner_ref,
    fock_ref,
    pair_ref,
    occ_ref,
    sems,
):
    moves = (
        (source_hbm, source_ref),
        (entry_hbm, entry_ref),
        (count_hbm, count_ref),
        (owner_hbm, owner_ref),
        (fock_hbm, fock_ref),
        (pair_hbm, pair_ref),
        (occ_hbm, occ_ref),
    )
    copies = [
        pltpu.make_async_copy(source, target, sems.at[k])
        for k, (source, target) in enumerate(moves)
    ]
    for copy in copies:
        copy.start()
    pairs = block_ref.shape[0]
    links = source_ref.shape[1]
    core = lax.axis_index("rep")
    row = lax.axis_index("pairs")
    peers = partners()

    columns = [coords_ref[p].T for p in range(pairs)]
    for p in range(pairs):
        for c in range(3):
            spread_ref[p, c] = jnp.broadcast_to(columns[p][:, c : c + 1], spread_ref.shape[2:])
        high_ref[p], low_ref[p] = split(overlap(columns[p], far_rows_ref[...]))
    zero = core == 0
    column = jnp.where(zero, columns[0], columns[1])
    energy = (column[:, 3:4] + coords_ref[core, 3:4, :]) * 0.5
    block = block_ref[core]
    metric = split(overlap(column, coords_ref[core]))
    firsts = [split(dot3(split(value), metric)) for value in (block, block * energy)]
    plain, scaled = [dot3(metric, first) for first in firsts]

    for copy in copies:
        copy.wait()

    def look(m, carry):
        own_slot, weights = carry
        weights = list(weights)
        for p in range(pairs):
            place = owner_ref[source_ref[p, m]]
            peer, _ = parts_of(place, pairs * sub_count)
            _, slot = parts_of(place, pairs)
            live = m < count_ref[p]
            value = fock_ref[entry_ref[p, m]]
            own = live & (peer == row)
            own_slot = jnp.where(own, slot, own_slot)
            for k, hit in enumerate((own, live & (peer == peers[0]), live & (peer == peers[1]))):
                weights[3 * p + k] += jnp.where(hit, value, 0.0)
        return own_slot, tuple(weights)

    shifts = [occ_ref[pair_ref[p, 0]] + occ_ref[pair_ref[p, 1]] for p in range(pairs)]
    shift = jnp.where(zero, shifts[0], shifts[1])
    share_ref[core] = integrals_ref[core] + scaled + plain * (energy - shift)
    own_slot, weights = lax.fori_loop(
        0, links, look, (jnp.int32(0), (jnp.float32(0.0),) * (3 * pairs))
    )
    for p in range(pairs):
        for k in range(2):
            weight_ref[k, p] = jnp.full((8, 128), weights[3 * p + 1 + k], jnp.float32)
        inverse_ref[p] = 1.0 / (columns[p][:, 3:4] + coords_ref[p, 3:4, :] - shifts[p])
    own_weight = jnp.where(zero, weights[0], weights[3])
    own = overlap(column, coords_ref[own_slot])
    share_ref[core] = share_ref[core] - own_weight * sandwich(own, block_ref[own_slot])
    share_ref[1 - core] = jnp.zeros_like(block)


def near_kernel(near_ref, wanted_ref, table_ref, spread_ref, weight_ref, share_ref, total_ref):
    pairs, size = share_ref.shape[0], share_ref.shape[1]
    half = size // 2
    near = jnp.where(jnp.max(wanted_ref[...]) > 0, near_ref[1], near_ref[0])
    part = split(near[:half, :])
    rows = jnp.concatenate(
        look_up(near[half : half + 1, :].astype(jnp.int32), table_ref, 3, 4), axis=0
    )
    metrics, firsts = [], []
    for p in range(pairs):
        left, right = overlap_spread(spread_ref, p, rows)
        metrics.append(split(jnp.concatenate([left, right], axis=1)))
        side = split(jnp.where(lax.axis_index("rep") == 0, left, right))
        firsts.append(split(dot3(side, part)))
    for p in range(pairs):
        term = dot3(firsts[p], metrics[p], NT)
        total_ref[p] = share_ref[p] - weight_ref[1, p, 0:1, 0:1] * term


def far_kernel(far_ref, high_ref, low_ref, weight_ref, share_ref, total_ref):
    pairs = share_ref.shape[0]
    block = split(far_ref[...])
    firsts = [split(dot3((high_ref[p], low_ref[p]), block)) for p in range(pairs)]
    for p in range(pairs):
        term = dot3(firsts[p], (high_ref[p], low_ref[p]), NT)
        total_ref[p] = share_ref[p] - weight_ref[0, p, 0:1, 0:1] * term


def final_kernel(
    share_ref, other_ref, block_ref, inverse_ref, residual_hbm, updated_hbm, residual_ref, updated_ref, sems
):
    copies = []
    for p in range(share_ref.shape[0]):
        residual = share_ref[p] + other_ref[p]
        residual_ref[p] = residual
        updated_ref[p] = block_ref[p] - residual * inverse_ref[p]
        for k, (source, target) in enumerate(
            ((residual_ref, residual_hbm), (updated_ref, updated_hbm))
        ):
            copies.append(pltpu.make_async_copy(source.at[p], target.at[p], sems.at[2 * p + k]))
            copies[-1].start()
    for copy in copies:
        copy.wait()


def call(
    body, outs, spaces, args, scratch=(), flops=0, moved=0, limit=VMEM_LIMIT, result=pltpu.VMEM
):
    return pl.pallas_call(
        body,
        out_shape=outs,
        in_specs=[pl.BlockSpec(memory_space=space) for space in spaces],
        out_specs=jax.tree.map(lambda _: pl.BlockSpec(memory_space=result), outs),
        scratch_shapes=list(scratch),
        compiler_params=pltpu.CompilerParams(vmem_limit_bytes=limit),
        cost_estimate=pl.CostEstimate(flops=flops, bytes_accessed=moved, transcendentals=0),
    )(*args)


def on_device_four(
    amplitudes,
    exchange_ints,
    pair_list,
    domains,
    link_source,
    link_entry,
    link_count,
    owner_map,
    fock_values,
    occ_energy,
    vir_energy,
    positions,
):
    pairs, size = amplitudes.shape[0], amplitudes.shape[1]
    sub_count = lax.axis_size("sub")
    core = lax.axis_index("rep")
    row = lax.axis_index("pairs")
    axes = ("pairs", "rep")
    across = [(2 * z + c, 2 * (z ^ (3 - c)) + c) for z in range(4) for c in range(2)]
    beside = [(2 * z + c, 2 * (z ^ 1) + c) for z in range(4) for c in range(2)]
    f32 = jnp.float32
    V, S = pltpu.VMEM, pltpu.SMEM

    opened = [
        pltpu.with_memory_space_constraint(value, pltpu.HBM)
        for value in (link_source, link_count, owner_map, domains, amplitudes)
    ]
    word = jax.ShapeDtypeStruct((8, 128), jnp.int32)
    message, wanted_near, halves = call(
        functools.partial(open_kernel, sub_count),
        (word, word, jax.ShapeDtypeStruct((pairs, size // 2 + COORD_ROWS, size), f32)),
        (pltpu.HBM,) * len(opened),
        opened,
        scratch=[
            V(link_source.shape, jnp.int32),
            S(link_count.shape, jnp.int32),
            S(owner_map.shape, jnp.int32),
            V(domains.shape, jnp.int32),
            pltpu.SemaphoreType.DMA((4 + pairs,)),
        ],
    )
    asked = lax.ppermute(message, axes, across)
    near = lax.ppermute(halves, axes, beside)
    block = jax.ShapeDtypeStruct((size, size), f32)
    far = call(select_kernel, block, (V, V), (asked, amplitudes), moved=10**6)
    far = lax.ppermute(far, axes, across)

    lines = -(-positions.shape[1] // 128)
    lines = -(-lines // 16) * 16
    coords, far_rows, table = call(
        centres_kernel,
        (
            jax.ShapeDtypeStruct((pairs, COORD_ROWS, size), f32),
            jax.ShapeDtypeStruct((COORD_ROWS, size), f32),
            jax.ShapeDtypeStruct((4 * lines, 128), f32),
        ),
        (pltpu.HBM, pltpu.HBM, V, V),
        (
            pltpu.with_memory_space_constraint(positions, pltpu.HBM),
            pltpu.with_memory_space_constraint(vir_energy, pltpu.HBM),
            message,
            asked,
        ),
        scratch=[
            V(positions.shape, f32),
            V(vir_energy.shape, f32),
            pltpu.SemaphoreType.DMA((2,)),
        ],
        flops=10**9,
        moved=10**6,
    )
    small = (
        link_source,
        link_entry,
        link_count,
        owner_map,
        fock_values,
        pair_list,
        occ_energy,
    )
    share, weight, inverse, spread, high, low = call(
        functools.partial(own_kernel, sub_count),
        (
            jax.ShapeDtypeStruct(amplitudes.shape, f32),
            jax.ShapeDtypeStruct((2, pairs, 8, 128), f32),
            jax.ShapeDtypeStruct(amplitudes.shape, f32),
            jax.ShapeDtypeStruct((pairs, 3, size, 128), f32),
            jax.ShapeDtypeStruct(amplitudes.shape, jnp.bfloat16),
            jax.ShapeDtypeStruct(amplitudes.shape, jnp.bfloat16),
        ),
        (V, V, V, V) + (pltpu.HBM,) * len(small),
        (
            amplitudes,
            exchange_ints,
            coords,
            far_rows,
            *(pltpu.with_memory_space_constraint(value, pltpu.HBM) for value in small),
        ),
        scratch=[S(value.shape, value.dtype) for value in small]
        + [pltpu.SemaphoreType.DMA((len(small),))],
        flops=2 * 10**10,
        moved=4 * 10**7,
    )
    whole = jax.ShapeDtypeStruct(amplitudes.shape, f32)
    cost = dict(flops=10**9, moved=10**6)
    share = call(
        near_kernel, whole, (V,) * 6, (near, wanted_near, table, spread, weight, share), **cost
    )
    share = call(far_kernel, whole, (V,) * 5, (far, high, low, weight, share), **cost)
    other = lax.ppermute(share, "rep", [(0, 1), (1, 0)])
    return call(
        final_kernel,
        (whole, whole),
        (V,) * 4,
        (share, other, amplitudes, inverse),
        scratch=[V(amplitudes.shape, f32), V(amplitudes.shape, f32), pltpu.SemaphoreType.DMA((2 * pairs,))],
        result=pltpu.HBM,
        **cost,
    )


def solution(mesh):
    stored = ("groups", "pairs", "sub")
    in_specs = (
        P(stored, None, None),
        P(stored, None, None),
        P(stored, None),
        P(stored, None),
        P(stored, None),
        P(stored, None),
        P(stored),
        P("groups"),
        P("groups"),
        P("groups"),
        P("groups"),
        P(None, "groups"),
    )
    out_specs = (P(stored, None, None), P(stored, None, None))

    def run(*args):
        devices = mesh.shape["groups"] * mesh.shape["pairs"] * mesh.shape["sub"]
        known = (
            mesh.shape["pairs"] == 4
            and mesh.shape["rep"] == 2
            and args[0].shape[0] == 2 * devices
            and args[0].shape[1] == 256
        )
        return jax.shard_map(
            on_device_four if known else on_device_any,
            mesh=mesh,
            in_specs=in_specs,
            out_specs=out_specs,
            check_vma=False,
        )(*args)

    return run
```

profile of v0, /device:TPU:19, one launch (start us, length us, event | category | flops | bytes accessed | tf_op | source)
XLA Modules:
  0.0 24.0 jit_solution(9396372332202304281)
XLA Ops:
  0.6 0.0 copy-start
  0.6 1.1 %shard_map.131 = (s32[8,128]{1,0:T(8,128)S(1)}, s32[8,128]{1,0:T(8,128)S(1)}, f32[2,136,256]{2,1,0:T(8,128)S(1)}) custom-call(s32[2,32]{1,0:T(2,128)} %source_hbm.3, s32[2]{0:T(128)} %count_hbm.3, s32[16]{0:T(128)} %owner_hbm.3, s32[2,256]{1,0:T(2,128)} %domains_hbm.1, f32[2,256,256]{2,1,0:T(8,128)} %block_ref.5), custom_call_target="tpu_custom_call" | custom-call | tf_op jit(solution)/shard_map/pallas_call | solution.py:465
  1.8 0.1 collective-permute-start
  1.9 1.3 %collective-permute-start.2 = (f32[2,136,256]{2,1,0:T(8,128)S(1)}, f32[2,136,256]{2,1,0:T(8,128)S(1)}, u32[]{:S(2)}, u32[]{:S(2)}) collective-permute-start(f32[2,136,256]{2,1,0:T(8,128)S(1)} %get-tuple-element.20), channel_id=1, source_target_pairs={{0,4},{1,5},{4,0},{5,1},{8,12},{9,13},{12,8},{13,9},{2,6},{3,7},{6... | collective-permute-start | bytes 835592 | tf_op jit(solution)/shard_map/ppermute | solution.py:519
  3.2 2.0 %collective-permute-done.asked_ref = s32[8,128]{1,0:T(8,128)S(1)} collective-permute-done((s32[8,128]{1,0:T(8,128)S(1)}, s32[8,128]{1,0:T(8,128)S(1)}, u32[]{:S(2)}, u32[]{:S(2)}) %collective-permute-start) | collective-permute-done | bytes 4128 | tf_op jit(solution)/shard_map/ppermute | solution.py:518
  5.2 0.0 copy-done
  5.2 0.0 copy-start.1
  5.2 0.4 %collective-permute-start.1 = (f32[256,256]{1,0:T(8,128)S(1)}, f32[256,256]{1,0:T(8,128)S(1)}, u32[]{:S(2)}, u32[]{:S(2)}) collective-permute-start(f32[256,256]{1,0:T(8,128)S(1)} %shard_map.132), channel_id=1, source_target_pairs={{0,12},{1,9},{4,8},{5,13},{8,4},{9,1},{12,0},{13,5},{2,14},{3,11},... | collective-permute-start | bytes 786440 | tf_op jit(solution)/shard_map/ppermute | solution.py:522
  5.6 2.1 %shard_map.133 = (f32[2,8,256]{2,1,0:T(8,128)S(1)}, f32[8,256]{1,0:T(8,128)S(1)}, f32[768,128]{1,0:T(8,128)S(1)}) custom-call(f32[3,24000]{1,0:T(4,128)} %positions_hbm.1, f32[24000]{0:T(1024)} %energy_hbm.1, s32[8,128]{1,0:T(8,128)S(1)} %get-tuple-element.14.message_ref, s32[8,128]{1,0:T(8,128)S(1)} %collective-permute-done.asked_ref), custom_call_target="tpu_custom_call" | custom-call | flops 1000000000 | bytes 1000000 | tf_op jit(solution)/shard_map/pallas_call | solution.py:465
  7.7 0.0 copy-done.1
  7.7 3.4 %shard_map.134 = (f32[2,256,256]{2,1,0:T(8,128)S(1)}, f32[2,2,8,128]{3,2,1,0:T(8,128)S(1)}, f32[2,256,256]{2,1,0:T(8,128)S(1)}, f32[2,3,256,128]{3,2,1,0:T(8,128...) custom-call(f32[2,256,256]{2,1,0:T(8,128)S(1)} %copy-done, f32[2,256,256]{2,1,0:T(8,128)S(1)} %copy-done.1, ...), custom_call_target="tpu_custom_call" | custom-call | flops 20000000000 | bytes 40000000 | tf_op jit(solution)/shard_map/pallas_call | solution.py:465
  11.1 0.0 collective-permute-done.2.near_ref
  11.1 1.4 %shard_map.135.share_ref = f32[2,256,256]{2,1,0:T(8,128)S(1)} custom-call(f32[2,136,256]{2,1,0:T(8,128)S(1)} %collective-permute-done.2.near_ref, s32[8,128]{1,0:T(8,128)S(1)} %get-tuple-element.21.wanted_ref, f32[768,128]{1,0:T(8,128)S(1)} %get-tuple-element.22.table_ref, f32[2,3,256,128]{3,2,1,0:T(8,128)S(1)} %get-tuple-element.23.spread_ref, ...), custom_call_target="tpu_custom_call" | custom-call | flops 1000000000 | bytes 1000000 | tf_op jit(solution)/shard_map/pallas_call | solution.py:465
  12.5 4.8 %collective-permute-done.1.far_ref = f32[256,256]{1,0:T(8,128)S(1)} collective-permute-done((f32[256,256]{1,0:T(8,128)S(1)}, f32[256,256]{1,0:T(8,128)S(1)}, u32[]{:S(2)}, u32[]{:S(2)}) %collective-permute-start.1) | collective-permute-done | bytes 262176 | tf_op jit(solution)/shard_map/ppermute | solution.py:522
  17.3 0.7 %shard_map.136.share_ref = f32[2,256,256]{2,1,0:T(8,128)S(1)} custom-call(f32[256,256]{1,0:T(8,128)S(1)} %collective-permute-done.1.far_ref, bf16[2,256,256]{2,1,0:T(8,128)(2,1)S(1)} %get-tuple-element.17.high_ref, bf16[2,256,256]{2,1,0:T(8,128)(2,1)S(1)} %get-tuple-element.18.low_ref, f32[2,2,8,128]{3,2,1,0:T(8,128)S(1)} %get-tuple-element.19.weight_ref, ...), custom_call_target="tpu_custom_call" | custom-call | flops 1000000000 | bytes 1000000 | tf_op jit(solution)/shard_map/pallas_call | solution.py:465
  18.0 3.5 %collective-permute-start.3 = (f32[2,256,256]{2,1,0:T(8,128)S(1)}, f32[2,256,256]{2,1,0:T(8,128)S(1)}, u32[]{:S(2)}, u32[]{:S(2)}) collective-permute-start(f32[2,256,256]{2,1,0:T(8,128)S(1)} %shard_map.136.share_ref), channel_id=1, source_target_pairs={{0,1},{1,0},{2,3},{3,2},{4,5},{5,4},{6,7},{7,6},{8,9},{9,8},{10,11... | collective-permute-start | bytes 1572872 | tf_op jit(solution)/shard_map/ppermute | solution.py:586
  21.5 1.5 %collective-permute-done.3.other_ref = f32[2,256,256]{2,1,0:T(8,128)S(1)} collective-permute-done((f32[2,256,256]{2,1,0:T(8,128)S(1)}, f32[2,256,256]{2,1,0:T(8,128)S(1)}, u32[]{:S(2)}, u32[]{:S(2)}) %collective-permute-start.3) | collective-permute-done | bytes 524320 | tf_op jit(solution)/shard_map/ppermute | solution.py:586
  23.0 1.0 %shard_map.137 = (f32[2,256,256]{2,1,0:T(8,128)}, f32[2,256,256]{2,1,0:T(8,128)}) custom-call(f32[2,256,256]{2,1,0:T(8,128)S(1)} %shard_map.136.share_ref, f32[2,256,256]{2,1,0:T(8,128)S(1)} %collective-permute-done.3.other_ref, f32[2,256,256]{2,1,0:T(8,128)S(1)} %copy-done, f32[2,256,256]{2,1,0:T(8,128)S(1)} %get-tuple-element.25.inverse_ref), custom_call_target="tpu_custom_call" | custom-call | flops 1000000000 | bytes 1000000 | tf_op jit(solution)/shard_map/pallas_call | solution.py:465
  (1 shorter events, 0.0 us)
Async XLA Ops:
  0.6 4.6 %copy-start = (f32[2,256,256]{2,1,0:T(8,128)S(1)}, f32[2,256,256]{2,1,0:T(8,128)}, u32[]{:S(2)}) copy-start(f32[2,256,256]{2,1,0:T(8,128)} %block_ref.5) | copy-start | bytes 1572868
  1.8 3.4 %collective-permute-start = (s32[8,128]{1,0:T(8,128)S(1)}, s32[8,128]{1,0:T(8,128)S(1)}, u32[]{:S(2)}, u32[]{:S(2)}) collective-permute-start(s32[8,128]{1,0:T(8,128)S(1)} %get-tuple-element.14.message_ref), channel_id=1, source_target_pairs={{0,12},{1,9},{4,8},{5,13},{8,4},{9,1},{12,0},{13,5},{2,14},{3,11},... | collective-permute-start | bytes 12296 | tf_op jit(solution)/shard_map/ppermute | solution.py:518
  1.9 9.2 %collective-permute-start.2 = (f32[2,136,256]{2,1,0:T(8,128)S(1)}, f32[2,136,256]{2,1,0:T(8,128)S(1)}, u32[]{:S(2)}, u32[]{:S(2)}) collective-permute-start(f32[2,136,256]{2,1,0:T(8,128)S(1)} %get-tuple-element.20), channel_id=1, source_target_pairs={{0,4},{1,5},{4,0},{5,1},{8,12},{9,13},{12,8},{13,9},{2,6},{3,7},{6... | collective-permute-start | bytes 835592 | tf_op jit(solution)/shard_map/ppermute | solution.py:519
  5.2 2.5 %copy-start.1 = (f32[2,256,256]{2,1,0:T(8,128)S(1)}, f32[2,256,256]{2,1,0:T(8,128)}, u32[]{:S(2)}) copy-start(f32[2,256,256]{2,1,0:T(8,128)} %integrals_ref.1) | copy-start | bytes 1572868
  5.2 12.1 %collective-permute-start.1 = (f32[256,256]{1,0:T(8,128)S(1)}, f32[256,256]{1,0:T(8,128)S(1)}, u32[]{:S(2)}, u32[]{:S(2)}) collective-permute-start(f32[256,256]{1,0:T(8,128)S(1)} %shard_map.132), channel_id=1, source_target_pairs={{0,12},{1,9},{4,8},{5,13},{8,4},{9,1},{12,0},{13,5},{2,14},{3,11},... | collective-permute-start | bytes 786440 | tf_op jit(solution)/shard_map/ppermute | solution.py:522
  18.0 5.1 %collective-permute-start.3 = (f32[2,256,256]{2,1,0:T(8,128)S(1)}, f32[2,256,256]{2,1,0:T(8,128)S(1)}, u32[]{:S(2)}, u32[]{:S(2)}) collective-permute-start(f32[2,256,256]{2,1,0:T(8,128)S(1)} %shard_map.136.share_ref), channel_id=1, source_target_pairs={{0,1},{1,0},{2,3},{3,2},{4,5},{5,4},{6,7},{7,6},{8,9},{9,8},{10,11... | collective-permute-start | bytes 1572872 | tf_op jit(solution)/shard_map/ppermute | solution.py:586
where the time goes:
time: 24.3 us; the launch traced here: 24 us
  Pallas kernels  9.69 us (40%)
  waiting for transfers between devices  8.3 us (34%)
  starting transfers between devices  5.34 us (22%)
  between operations  0.71 us (3%)
    pallas_call x7, Pallas kernels, call(): pl.pallas_call(body, out_shape=outs, in_specs=[pl.BlockSpec(memory_space=...  9.69 us
    ppermute x1, waiting for transfers between devices, on_device_four(): far = lax.ppermute(far, axes, across)  4.78 us
    ppermute x1, starting transfers between devices, on_device_four(): other = lax.ppermute(share, 'rep', [(0, 1), (1, 0)])  3.53 us
    ppermute x1, waiting for transfers between devices, on_device_four(): asked = lax.ppermute(message, axes, across)  1.98 us
    ppermute x1, waiting for transfers between devices, on_device_four(): other = lax.ppermute(share, 'rep', [(0, 1), (1, 0)])  1.54 us
    ppermute x1, starting transfers between devices, on_device_four(): near = lax.ppermute(halves, axes, beside)  1.32 us
  transfers between devices with their start and end apart: 4, of which 3 were waited for; matrix products, arithmetic and copies ran while one was open for 0% of the time, Pallas kernels for 29%

commit v1 on v0

--- a/solution.py
+++ b/solution.py
@@ -167,9 +167,16 @@
     return lax.div(value, divisor), lax.rem(value, divisor)
 
 
+def outer_core(row):
+    return 1 if row in (1,) else 0
+
+
 def partners():
     row = lax.axis_index("pairs")
-    return row ^ (3 - lax.axis_index("rep")), row ^ 1
+    outer = jnp.int32(0)
+    for z in range(4):
+        outer = jnp.where(row == z, outer_core(z), outer)
+    return jnp.where(lax.axis_index("rep") == outer, row ^ 3, row ^ 2), row ^ 1
 
 
 def open_kernel(
@@ -492,7 +499,8 @@
     core = lax.axis_index("rep")
     row = lax.axis_index("pairs")
     axes = ("pairs", "rep")
-    across = [(2 * z + c, 2 * (z ^ (3 - c)) + c) for z in range(4) for c in range(2)]
+    across = [(2 * z + outer_core(z), 2 * (z ^ 3) + outer_core(z ^ 3)) for z in range(4)]
+    across += [(2 * z + 1 - outer_core(z), 2 * (z ^ 2) + 1 - outer_core(z ^ 2)) for z in range(4)]
     beside = [(2 * z + c, 2 * (z ^ 1) + c) for z in range(4) for c in range(2)]
     f32 = jnp.float32
     V, S = pltpu.VMEM, pltpu.SMEM

time: 24.3 us -> 24.1 us (level)
  the two profiles are of different devices: /device:TPU:19 before, /device:TPU:0 now
where the time goes in v1:
time: 24.1 us; the launch traced here: 23.9 us
  starting transfers between devices  9.77 us (41%)
  Pallas kernels  9.69 us (40%)
  waiting for transfers between devices  3.73 us (15%)
  between operations  0.71 us (3%)
    pallas_call x7, Pallas kernels, call(): pl.pallas_call(body, out_shape=outs, in_specs=[pl.BlockSpec(memory_space=...  9.69 us
    ppermute x1, starting transfers between devices, on_device_four(): asked = lax.ppermute(message, axes, across)  5.11 us
    ppermute x1, starting transfers between devices, on_device_four(): far = lax.ppermute(far, axes, across)  3.92 us
    ppermute x1, waiting for transfers between devices, on_device_four(): asked = lax.ppermute(message, axes, across)  1.63 us
    ppermute x1, waiting for transfers between devices, on_device_four(): other = lax.ppermute(share, 'rep', [(0, 1), (1, 0)])  1.54 us
    ppermute x1, starting transfers between devices, on_device_four(): other = lax.ppermute(share, 'rep', [(0, 1), (1, 0)])  0.73 us
    ppermute x1, waiting for transfers between devices, on_device_four(): far = lax.ppermute(far, axes, across)  0.56 us
  transfers between devices with their start and end apart: 4, of which 3 were waited for; matrix products, arithmetic and copies ran while one was open for 0% of the time, Pallas kernels for 29%

profile of v1, /device:TPU:0, one launch (start us, length us, event | category | flops | bytes accessed | tf_op | source)
XLA Modules:
  0.0 23.9 jit_solution(614867195179880377)
XLA Ops:
  0.6 0.0 copy-start
  0.6 1.1 %shard_map.131 = (s32[8,128]{1,0:T(8,128)S(1)}, s32[8,128]{1,0:T(8,128)S(1)}, f32[2,136,256]{2,1,0:T(8,128)S(1)}) custom-call(s32[2,32]{1,0:T(2,128)} %source_hbm.3, s32[2]{0:T(128)} %count_hbm.3, s32[16]{0:T(128)} %owner_hbm.3, s32[2,256]{1,0:T(2,128)} %domains_hbm.1, f32[2,256,256]{2,1,0:T(8,128)} %block_ref.5), custom_call_target="tpu_custom_call" | custom-call | tf_op jit(solution)/shard_map/pallas_call | solution.py:472
  1.8 5.1 %collective-permute-start = (s32[8,128]{1,0:T(8,128)S(1)}, s32[8,128]{1,0:T(8,128)S(1)}, u32[]{:S(2)}, u32[]{:S(2)}) collective-permute-start(s32[8,128]{1,0:T(8,128)S(1)} %get-tuple-element.14.message_ref), channel_id=1, source_target_pairs={{0,12},{5,8},{8,5},{12,0},{1,9},{4,13},{9,1},{13,4},{2,14},{7,10},... | collective-permute-start | bytes 12296 | tf_op jit(solution)/shard_map/ppermute | solution.py:526
  6.9 0.0 collective-permute-start.2
  6.9 1.6 %collective-permute-done.asked_ref = s32[8,128]{1,0:T(8,128)S(1)} collective-permute-done((s32[8,128]{1,0:T(8,128)S(1)}, s32[8,128]{1,0:T(8,128)S(1)}, u32[]{:S(2)}, u32[]{:S(2)}) %collective-permute-start) | collective-permute-done | bytes 4128 | tf_op jit(solution)/shard_map/ppermute | solution.py:526
  8.5 0.0 copy-done
  8.5 0.0 copy-start.1
  8.6 3.9 %collective-permute-start.1 = (f32[256,256]{1,0:T(8,128)S(1)}, f32[256,256]{1,0:T(8,128)S(1)}, u32[]{:S(2)}, u32[]{:S(2)}) collective-permute-start(f32[256,256]{1,0:T(8,128)S(1)} %shard_map.132), channel_id=1, source_target_pairs={{0,12},{5,8},{8,5},{12,0},{1,9},{4,13},{9,1},{13,4},{2,14},{7,10},... | collective-permute-start | bytes 786440 | tf_op jit(solution)/shard_map/ppermute | solution.py:530
  12.5 2.1 %shard_map.133 = (f32[2,8,256]{2,1,0:T(8,128)S(1)}, f32[8,256]{1,0:T(8,128)S(1)}, f32[768,128]{1,0:T(8,128)S(1)}) custom-call(f32[3,24000]{1,0:T(4,128)} %positions_hbm.1, f32[24000]{0:T(1024)} %energy_hbm.1, s32[8,128]{1,0:T(8,128)S(1)} %get-tuple-element.14.message_ref, s32[8,128]{1,0:T(8,128)S(1)} %collective-permute-done.asked_ref), custom_call_target="tpu_custom_call" | custom-call | flops 1000000000 | bytes 1000000 | tf_op jit(solution)/shard_map/pallas_call | solution.py:472
  14.6 0.0 copy-done.1
  14.6 3.4 %shard_map.134 = (f32[2,256,256]{2,1,0:T(8,128)S(1)}, f32[2,2,8,128]{3,2,1,0:T(8,128)S(1)}, f32[2,256,256]{2,1,0:T(8,128)S(1)}, f32[2,3,256,128]{3,2,1,0:T(8,128...) custom-call(f32[2,256,256]{2,1,0:T(8,128)S(1)} %copy-done, f32[2,256,256]{2,1,0:T(8,128)S(1)} %copy-done.1, ...), custom_call_target="tpu_custom_call" | custom-call | flops 20000000000 | bytes 40000000 | tf_op jit(solution)/shard_map/pallas_call | solution.py:472
  18.0 0.0 collective-permute-done.2.near_ref
  18.0 1.4 %shard_map.135.share_ref = f32[2,256,256]{2,1,0:T(8,128)S(1)} custom-call(f32[2,136,256]{2,1,0:T(8,128)S(1)} %collective-permute-done.2.near_ref, s32[8,128]{1,0:T(8,128)S(1)} %get-tuple-element.21.wanted_ref, f32[768,128]{1,0:T(8,128)S(1)} %get-tuple-element.22.table_ref, f32[2,3,256,128]{3,2,1,0:T(8,128)S(1)} %get-tuple-element.23.spread_ref, ...), custom_call_target="tpu_custom_call" | custom-call | flops 1000000000 | bytes 1000000 | tf_op jit(solution)/shard_map/pallas_call | solution.py:472
  19.4 0.6 %collective-permute-done.1.far_ref = f32[256,256]{1,0:T(8,128)S(1)} collective-permute-done((f32[256,256]{1,0:T(8,128)S(1)}, f32[256,256]{1,0:T(8,128)S(1)}, u32[]{:S(2)}, u32[]{:S(2)}) %collective-permute-start.1) | collective-permute-done | bytes 262176 | tf_op jit(solution)/shard_map/ppermute | solution.py:530
  19.9 0.7 %shard_map.136.share_ref = f32[2,256,256]{2,1,0:T(8,128)S(1)} custom-call(f32[256,256]{1,0:T(8,128)S(1)} %collective-permute-done.1.far_ref, bf16[2,256,256]{2,1,0:T(8,128)(2,1)S(1)} %get-tuple-element.17.high_ref, bf16[2,256,256]{2,1,0:T(8,128)(2,1)S(1)} %get-tuple-element.18.low_ref, f32[2,2,8,128]{3,2,1,0:T(8,128)S(1)} %get-tuple-element.19.weight_ref, ...), custom_call_target="tpu_custom_call" | custom-call | flops 1000000000 | bytes 1000000 | tf_op jit(solution)/shard_map/pallas_call | solution.py:472
  20.6 0.7 %collective-permute-start.3 = (f32[2,256,256]{2,1,0:T(8,128)S(1)}, f32[2,256,256]{2,1,0:T(8,128)S(1)}, u32[]{:S(2)}, u32[]{:S(2)}) collective-permute-start(f32[2,256,256]{2,1,0:T(8,128)S(1)} %shard_map.136.share_ref), channel_id=1, source_target_pairs={{0,1},{1,0},{2,3},{3,2},{4,5},{5,4},{6,7},{7,6},{8,9},{9,8},{10,11... | collective-permute-start | bytes 1572872 | tf_op jit(solution)/shard_map/ppermute | solution.py:594
  21.3 1.5 %collective-permute-done.3.other_ref = f32[2,256,256]{2,1,0:T(8,128)S(1)} collective-permute-done((f32[2,256,256]{2,1,0:T(8,128)S(1)}, f32[2,256,256]{2,1,0:T(8,128)S(1)}, u32[]{:S(2)}, u32[]{:S(2)}) %collective-permute-start.3) | collective-permute-done | bytes 524320 | tf_op jit(solution)/shard_map/ppermute | solution.py:594
  22.9 1.0 %shard_map.137 = (f32[2,256,256]{2,1,0:T(8,128)}, f32[2,256,256]{2,1,0:T(8,128)}) custom-call(f32[2,256,256]{2,1,0:T(8,128)S(1)} %shard_map.136.share_ref, f32[2,256,256]{2,1,0:T(8,128)S(1)} %collective-permute-done.3.other_ref, f32[2,256,256]{2,1,0:T(8,128)S(1)} %copy-done, f32[2,256,256]{2,1,0:T(8,128)S(1)} %get-tuple-element.25.inverse_ref), custom_call_target="tpu_custom_call" | custom-call | flops 1000000000 | bytes 1000000 | tf_op jit(solution)/shard_map/pallas_call | solution.py:472
  (1 shorter events, 0.0 us)
Async XLA Ops:
  0.6 7.9 %copy-start = (f32[2,256,256]{2,1,0:T(8,128)S(1)}, f32[2,256,256]{2,1,0:T(8,128)}, u32[]{:S(2)}) copy-start(f32[2,256,256]{2,1,0:T(8,128)} %block_ref.5) | copy-start | bytes 1572868
  1.8 6.7 %collective-permute-start = (s32[8,128]{1,0:T(8,128)S(1)}, s32[8,128]{1,0:T(8,128)S(1)}, u32[]{:S(2)}, u32[]{:S(2)}) collective-permute-start(s32[8,128]{1,0:T(8,128)S(1)} %get-tuple-element.14.message_ref), channel_id=1, source_target_pairs={{0,12},{5,8},{8,5},{12,0},{1,9},{4,13},{9,1},{13,4},{2,14},{7,10},... | collective-permute-start | bytes 12296 | tf_op jit(solution)/shard_map/ppermute | solution.py:526
  6.9 11.1 %collective-permute-start.2 = (f32[2,136,256]{2,1,0:T(8,128)S(1)}, f32[2,136,256]{2,1,0:T(8,128)S(1)}, u32[]{:S(2)}, u32[]{:S(2)}) collective-permute-start(f32[2,136,256]{2,1,0:T(8,128)S(1)} %get-tuple-element.20), channel_id=1, source_target_pairs={{0,4},{1,5},{4,0},{5,1},{8,12},{9,13},{12,8},{13,9},{2,6},{3,7},{6... | collective-permute-start | bytes 835592 | tf_op jit(solution)/shard_map/ppermute | solution.py:527
  8.5 6.1 %copy-start.1 = (f32[2,256,256]{2,1,0:T(8,128)S(1)}, f32[2,256,256]{2,1,0:T(8,128)}, u32[]{:S(2)}) copy-start(f32[2,256,256]{2,1,0:T(8,128)} %integrals_ref.1) | copy-start | bytes 1572868
  8.6 11.4 %collective-permute-start.1 = (f32[256,256]{1,0:T(8,128)S(1)}, f32[256,256]{1,0:T(8,128)S(1)}, u32[]{:S(2)}, u32[]{:S(2)}) collective-permute-start(f32[256,256]{1,0:T(8,128)S(1)} %shard_map.132), channel_id=1, source_target_pairs={{0,12},{5,8},{8,5},{12,0},{1,9},{4,13},{9,1},{13,4},{2,14},{7,10},... | collective-permute-start | bytes 786440 | tf_op jit(solution)/shard_map/ppermute | solution.py:530
  20.6 2.3 %collective-permute-start.3 = (f32[2,256,256]{2,1,0:T(8,128)S(1)}, f32[2,256,256]{2,1,0:T(8,128)S(1)}, u32[]{:S(2)}, u32[]{:S(2)}) collective-permute-start(f32[2,256,256]{2,1,0:T(8,128)S(1)} %shard_map.136.share_ref), channel_id=1, source_target_pairs={{0,1},{1,0},{2,3},{3,2},{4,5},{5,4},{6,7},{7,6},{8,9},{9,8},{10,11... | collective-permute-start | bytes 1572872 | tf_op jit(solution)/shard_map/ppermute | solution.py:594

commit v2 on v1

--- a/solution.py
+++ b/solution.py
@@ -206,7 +206,7 @@
         (domains_hbm, domains_ref),
     ]
     moves += [
-        (block_hbm.at[p, pl.ds(start, half), :], halves_ref.at[p, pl.ds(0, half), :])
+        (block_hbm.at[p, pl.ds(start, half), :], halves_ref.at[pl.ds(p * half, half), :])
         for p in range(pairs)
     ]
     copies = [
@@ -235,9 +235,9 @@
         for k in range(2):
             row = 4 + 2 * p + k
             message_ref[row : row + 1, :] = domains_ref[p : p + 1, k * 128 : (k + 1) * 128]
-        halves_ref[p, half:, :] = jnp.broadcast_to(
-            domains_ref[p : p + 1, :].astype(jnp.float32), (COORD_ROWS, size)
-        )
+    names = domains_ref[...].astype(jnp.float32)
+    blank = jnp.zeros((COORD_ROWS - pairs, size), jnp.float32)
+    halves_ref[pairs * half :, :] = jnp.concatenate([names, blank], axis=0)
     for copy in copies[4:]:
         copy.wait()
 
@@ -424,10 +424,13 @@
 def near_kernel(near_ref, wanted_ref, table_ref, spread_ref, weight_ref, share_ref, total_ref):
     pairs, size = share_ref.shape[0], share_ref.shape[1]
     half = size // 2
-    near = jnp.where(jnp.max(wanted_ref[...]) > 0, near_ref[1], near_ref[0])
-    part = split(near[:half, :])
+    slot_one = jnp.max(wanted_ref[...]) > 0
+    part = split(jnp.where(slot_one, near_ref[half : 2 * half, :], near_ref[:half, :]))
+    names = jnp.where(
+        slot_one, near_ref[2 * half + 1 : 2 * half + 2, :], near_ref[2 * half : 2 * half + 1, :]
+    )
     rows = jnp.concatenate(
-        look_up(near[half : half + 1, :].astype(jnp.int32), table_ref, 3, 4), axis=0
+        look_up(names.astype(jnp.int32), table_ref, 3, 4), axis=0
     )
     metrics, firsts = [], []
     for p in range(pairs):
@@ -512,7 +515,7 @@
     word = jax.ShapeDtypeStruct((8, 128), jnp.int32)
     message, wanted_near, halves = call(
         functools.partial(open_kernel, sub_count),
-        (word, word, jax.ShapeDtypeStruct((pairs, size // 2 + COORD_ROWS, size), f32)),
+        (word, word, jax.ShapeDtypeStruct((pairs * size // 2 + COORD_ROWS, size), f32)),
         (pltpu.HBM,) * len(opened),
         opened,
         scratch=[

time: 24.1 us -> 24.1 us (level)
  no operation moved by 1% of the time
where the time goes in v2:
time: 24.1 us; the launch traced here: 23.9 us
  starting transfers between devices  9.95 us (41%)
  Pallas kernels  9.7 us (40%)
  waiting for transfers between devices  3.54 us (15%)
  between operations  0.71 us (3%)
    pallas_call x7, Pallas kernels, call(): pl.pallas_call(body, out_shape=outs, in_specs=[pl.BlockSpec(memory_space=...  9.7 us
    ppermute x1, starting transfers between devices, on_device_four(): asked = lax.ppermute(message, axes, across)  5.11 us
    ppermute x1, starting transfers between devices, on_device_four(): far = lax.ppermute(far, axes, across)  3.92 us
    ppermute x1, waiting for transfers between devices, on_device_four(): asked = lax.ppermute(message, axes, across)  1.63 us
    ppermute x1, waiting for transfers between devices, on_device_four(): other = lax.ppermute(share, 'rep', [(0, 1), (1, 0)])  1.54 us
    ppermute x1, starting transfers between devices, on_device_four(): other = lax.ppermute(share, 'rep', [(0, 1), (1, 0)])  0.91 us
  transfers between devices with their start and end apart: 4, of which 3 were waited for; matrix products, arithmetic and copies ran while one was open for 0% of the time, Pallas kernels for 29%

profile of v2, /device:TPU:0, one launch (start us, length us, event | category | flops | bytes accessed | tf_op | source)
XLA Modules:
  0.0 23.9 jit_solution(16763297593537472277)
XLA Ops:
  0.6 0.0 copy-start
  0.6 1.1 %shard_map.131 = (s32[8,128]{1,0:T(8,128)S(1)}, s32[8,128]{1,0:T(8,128)S(1)}, f32[264,256]{1,0:T(8,128)S(1)}) custom-call(s32[2,32]{1,0:T(2,128)} %source_hbm.3, s32[2]{0:T(128)} %count_hbm.3, s32[16]{0:T(128)} %owner_hbm.3, s32[2,256]{1,0:T(2,128)} %domains_hbm.1, f32[2,256,256]{2,1,0:T(8,128)} %block_ref.5), custom_call_target="tpu_custom_call" | custom-call | tf_op jit(solution)/shard_map/pallas_call | solution.py:475
  1.8 5.1 %collective-permute-start = (s32[8,128]{1,0:T(8,128)S(1)}, s32[8,128]{1,0:T(8,128)S(1)}, u32[]{:S(2)}, u32[]{:S(2)}) collective-permute-start(s32[8,128]{1,0:T(8,128)S(1)} %get-tuple-element.14.message_ref), channel_id=1, source_target_pairs={{0,12},{5,8},{8,5},{12,0},{1,9},{4,13},{9,1},{13,4},{2,14},{7,10},... | collective-permute-start | bytes 12296 | tf_op jit(solution)/shard_map/ppermute | solution.py:529
  6.9 0.0 collective-permute-start.2
  6.9 1.6 %collective-permute-done.asked_ref = s32[8,128]{1,0:T(8,128)S(1)} collective-permute-done((s32[8,128]{1,0:T(8,128)S(1)}, s32[8,128]{1,0:T(8,128)S(1)}, u32[]{:S(2)}, u32[]{:S(2)}) %collective-permute-start) | collective-permute-done | bytes 4128 | tf_op jit(solution)/shard_map/ppermute | solution.py:529
  8.5 0.0 copy-done
  8.5 0.0 copy-start.1
  8.6 3.9 %collective-permute-start.1 = (f32[256,256]{1,0:T(8,128)S(1)}, f32[256,256]{1,0:T(8,128)S(1)}, u32[]{:S(2)}, u32[]{:S(2)}) collective-permute-start(f32[256,256]{1,0:T(8,128)S(1)} %shard_map.132), channel_id=1, source_target_pairs={{0,12},{5,8},{8,5},{12,0},{1,9},{4,13},{9,1},{13,4},{2,14},{7,10},... | collective-permute-start | bytes 786440 | tf_op jit(solution)/shard_map/ppermute | solution.py:533
  12.5 2.1 %shard_map.133 = (f32[2,8,256]{2,1,0:T(8,128)S(1)}, f32[8,256]{1,0:T(8,128)S(1)}, f32[768,128]{1,0:T(8,128)S(1)}) custom-call(f32[3,24000]{1,0:T(4,128)} %positions_hbm.1, f32[24000]{0:T(1024)} %energy_hbm.1, s32[8,128]{1,0:T(8,128)S(1)} %get-tuple-element.14.message_ref, s32[8,128]{1,0:T(8,128)S(1)} %collective-permute-done.asked_ref), custom_call_target="tpu_custom_call" | custom-call | flops 1000000000 | bytes 1000000 | tf_op jit(solution)/shard_map/pallas_call | solution.py:475
  14.6 0.0 copy-done.1
  14.6 3.4 %shard_map.134 = (f32[2,256,256]{2,1,0:T(8,128)S(1)}, f32[2,2,8,128]{3,2,1,0:T(8,128)S(1)}, f32[2,256,256]{2,1,0:T(8,128)S(1)}, f32[2,3,256,128]{3,2,1,0:T(8,128...) custom-call(f32[2,256,256]{2,1,0:T(8,128)S(1)} %copy-done, f32[2,256,256]{2,1,0:T(8,128)S(1)} %copy-done.1, ...), custom_call_target="tpu_custom_call" | custom-call | flops 20000000000 | bytes 40000000 | tf_op jit(solution)/shard_map/pallas_call | solution.py:475
  18.0 0.0 collective-permute-done.2.near_ref
  18.0 1.4 %shard_map.135.share_ref = f32[2,256,256]{2,1,0:T(8,128)S(1)} custom-call(f32[264,256]{1,0:T(8,128)S(1)} %collective-permute-done.2.near_ref, s32[8,128]{1,0:T(8,128)S(1)} %get-tuple-element.21.wanted_ref, f32[768,128]{1,0:T(8,128)S(1)} %get-tuple-element.22.table_ref, f32[2,3,256,128]{3,2,1,0:T(8,128)S(1)} %get-tuple-element.23.spread_ref, ...), custom_call_target="tpu_custom_call" | custom-call | flops 1000000000 | bytes 1000000 | tf_op jit(solution)/shard_map/pallas_call | solution.py:475
  19.4 0.4 %collective-permute-done.1.far_ref = f32[256,256]{1,0:T(8,128)S(1)} collective-permute-done((f32[256,256]{1,0:T(8,128)S(1)}, f32[256,256]{1,0:T(8,128)S(1)}, u32[]{:S(2)}, u32[]{:S(2)}) %collective-permute-start.1) | collective-permute-done | bytes 262176 | tf_op jit(solution)/shard_map/ppermute | solution.py:533
  19.8 0.7 %shard_map.136.share_ref = f32[2,256,256]{2,1,0:T(8,128)S(1)} custom-call(f32[256,256]{1,0:T(8,128)S(1)} %collective-permute-done.1.far_ref, bf16[2,256,256]{2,1,0:T(8,128)(2,1)S(1)} %get-tuple-element.17.high_ref, bf16[2,256,256]{2,1,0:T(8,128)(2,1)S(1)} %get-tuple-element.18.low_ref, f32[2,2,8,128]{3,2,1,0:T(8,128)S(1)} %get-tuple-element.19.weight_ref, ...), custom_call_target="tpu_custom_call" | custom-call | flops 1000000000 | bytes 1000000 | tf_op jit(solution)/shard_map/pallas_call | solution.py:475
  20.4 0.9 %collective-permute-start.3 = (f32[2,256,256]{2,1,0:T(8,128)S(1)}, f32[2,256,256]{2,1,0:T(8,128)S(1)}, u32[]{:S(2)}, u32[]{:S(2)}) collective-permute-start(f32[2,256,256]{2,1,0:T(8,128)S(1)} %shard_map.136.share_ref), channel_id=1, source_target_pairs={{0,1},{1,0},{2,3},{3,2},{4,5},{5,4},{6,7},{7,6},{8,9},{9,8},{10,11... | collective-permute-start | bytes 1572872 | tf_op jit(solution)/shard_map/ppermute | solution.py:597
  21.3 1.5 %collective-permute-done.3.other_ref = f32[2,256,256]{2,1,0:T(8,128)S(1)} collective-permute-done((f32[2,256,256]{2,1,0:T(8,128)S(1)}, f32[2,256,256]{2,1,0:T(8,128)S(1)}, u32[]{:S(2)}, u32[]{:S(2)}) %collective-permute-start.3) | collective-permute-done | bytes 524320 | tf_op jit(solution)/shard_map/ppermute | solution.py:597
  22.9 1.0 %shard_map.137 = (f32[2,256,256]{2,1,0:T(8,128)}, f32[2,256,256]{2,1,0:T(8,128)}) custom-call(f32[2,256,256]{2,1,0:T(8,128)S(1)} %shard_map.136.share_ref, f32[2,256,256]{2,1,0:T(8,128)S(1)} %collective-permute-done.3.other_ref, f32[2,256,256]{2,1,0:T(8,128)S(1)} %copy-done, f32[2,256,256]{2,1,0:T(8,128)S(1)} %get-tuple-element.25.inverse_ref), custom_call_target="tpu_custom_call" | custom-call | flops 1000000000 | bytes 1000000 | tf_op jit(solution)/shard_map/pallas_call | solution.py:475
  (1 shorter events, 0.0 us)
Async XLA Ops:
  0.6 7.9 %copy-start = (f32[2,256,256]{2,1,0:T(8,128)S(1)}, f32[2,256,256]{2,1,0:T(8,128)}, u32[]{:S(2)}) copy-start(f32[2,256,256]{2,1,0:T(8,128)} %block_ref.5) | copy-start | bytes 1572868
  1.8 6.7 %collective-permute-start = (s32[8,128]{1,0:T(8,128)S(1)}, s32[8,128]{1,0:T(8,128)S(1)}, u32[]{:S(2)}, u32[]{:S(2)}) collective-permute-start(s32[8,128]{1,0:T(8,128)S(1)} %get-tuple-element.14.message_ref), channel_id=1, source_target_pairs={{0,12},{5,8},{8,5},{12,0},{1,9},{4,13},{9,1},{13,4},{2,14},{7,10},... | collective-permute-start | bytes 12296 | tf_op jit(solution)/shard_map/ppermute | solution.py:529
  6.9 11.1 %collective-permute-start.2 = (f32[264,256]{1,0:T(8,128)S(1)}, f32[264,256]{1,0:T(8,128)S(1)}, u32[]{:S(2)}, u32[]{:S(2)}) collective-permute-start(f32[264,256]{1,0:T(8,128)S(1)} %get-tuple-element.20), channel_id=1, source_target_pairs={{0,4},{1,5},{4,0},{5,1},{8,12},{9,13},{12,8},{13,9},{2,6},{3,7},{6... | collective-permute-start | bytes 811016 | tf_op jit(solution)/shard_map/ppermute | solution.py:530
  8.5 6.1 %copy-start.1 = (f32[2,256,256]{2,1,0:T(8,128)S(1)}, f32[2,256,256]{2,1,0:T(8,128)}, u32[]{:S(2)}) copy-start(f32[2,256,256]{2,1,0:T(8,128)} %integrals_ref.1) | copy-start | bytes 1572868
  8.6 11.2 %collective-permute-start.1 = (f32[256,256]{1,0:T(8,128)S(1)}, f32[256,256]{1,0:T(8,128)S(1)}, u32[]{:S(2)}, u32[]{:S(2)}) collective-permute-start(f32[256,256]{1,0:T(8,128)S(1)} %shard_map.132), channel_id=1, source_target_pairs={{0,12},{5,8},{8,5},{12,0},{1,9},{4,13},{9,1},{13,4},{2,14},{7,10},... | collective-permute-start | bytes 786440 | tf_op jit(solution)/shard_map/ppermute | solution.py:533
  20.4 2.4 %collective-permute-start.3 = (f32[2,256,256]{2,1,0:T(8,128)S(1)}, f32[2,256,256]{2,1,0:T(8,128)S(1)}, u32[]{:S(2)}, u32[]{:S(2)}) collective-permute-start(f32[2,256,256]{2,1,0:T(8,128)S(1)} %shard_map.136.share_ref), channel_id=1, source_target_pairs={{0,1},{1,0},{2,3},{3,2},{4,5},{5,4},{6,7},{7,6},{8,9},{9,8},{10,11... | collective-permute-start | bytes 1572872 | tf_op jit(solution)/shard_map/ppermute | solution.py:597

commit v3 on v2

--- a/solution.py
+++ b/solution.py
@@ -307,7 +307,7 @@
         table[3 * rows + whole : 3 * rows + whole + 1, :rest] = energy_ref[whole * 128 :].reshape(
             1, rest
         )
-    slot_one = jnp.max(message_ref[0:1, :]) > 0
+    slot_one = jnp.concatenate([message_ref[0:1, :]] * (size // 128), axis=1) > 0
     index = [domain_of(message_ref, p) for p in range(pairs)]
     index.append(jnp.where(slot_one, domain_of(asked_ref, 1), domain_of(asked_ref, 0)))
     found = look_up(jnp.concatenate(index, axis=1), table, 4, 4)
@@ -424,7 +424,7 @@
 def near_kernel(near_ref, wanted_ref, table_ref, spread_ref, weight_ref, share_ref, total_ref):
     pairs, size = share_ref.shape[0], share_ref.shape[1]
     half = size // 2
-    slot_one = jnp.max(wanted_ref[...]) > 0
+    slot_one = jnp.concatenate([wanted_ref[0:1, :]] * (size // 128), axis=1) > 0
     part = split(jnp.where(slot_one, near_ref[half : 2 * half, :], near_ref[:half, :]))
     names = jnp.where(
         slot_one, near_ref[2 * half + 1 : 2 * half + 2, :], near_ref[2 * half : 2 * half + 1, :]

time: 24.1 us -> 24.1 us (level)
  Pallas kernels: 9.7 us -> 9.44 us
  waiting for transfers between devices: 3.54 us -> 3.8 us
    ppermute x1, waiting for transfers between devices: 0.38 us -> 0.64 us  [on_device_four(): far = lax.ppermute(far, axes, across)]
    pallas_call x7, Pallas kernels: 9.7 us -> 9.44 us  [call(): pl.pallas_call(body, out_shape=outs, in_specs=[pl.BlockSpec(memory_space=...]
  transfers between devices with their start and end apart: 4 -> 4, of which waited for: 3 -> 3; matrix products, arithmetic and copies ran while one was open for 0% -> 0% of each run, Pallas kernels for 29% -> 28%
where the time goes in v3:
time: 24.1 us; the launch traced here: 23.9 us
  starting transfers between devices  9.95 us (41%)
  Pallas kernels  9.44 us (39%)
  waiting for transfers between devices  3.8 us (16%)
  between operations  0.71 us (3%)
    pallas_call x7, Pallas kernels, call(): pl.pallas_call(body, out_shape=outs, in_specs=[pl.BlockSpec(memory_space=...  9.44 us
    ppermute x1, starting transfers between devices, on_device_four(): asked = lax.ppermute(message, axes, across)  5.11 us
    ppermute x1, starting transfers between devices, on_device_four(): far = lax.ppermute(far, axes, across)  3.92 us
    ppermute x1, waiting for transfers between devices, on_device_four(): asked = lax.ppermute(message, axes, across)  1.63 us
    ppermute x1, waiting for transfers between devices, on_device_four(): other = lax.ppermute(share, 'rep', [(0, 1), (1, 0)])  1.54 us
    ppermute x1, starting transfers between devices, on_device_four(): other = lax.ppermute(share, 'rep', [(0, 1), (1, 0)])  0.91 us
    ppermute x1, waiting for transfers between devices, on_device_four(): far = lax.ppermute(far, axes, across)  0.64 us
  transfers between devices with their start and end apart: 4, of which 3 were waited for; matrix products, arithmetic and copies ran while one was open for 0% of the time, Pallas kernels for 28%

profile of v3, /device:TPU:0, one launch (start us, length us, event | category | flops | bytes accessed | tf_op | source)
XLA Modules:
  0.0 23.9 jit_solution(18087887646853346475)
XLA Ops:
  0.6 0.0 copy-start
  0.6 1.1 %shard_map.131 = (s32[8,128]{1,0:T(8,128)S(1)}, s32[8,128]{1,0:T(8,128)S(1)}, f32[264,256]{1,0:T(8,128)S(1)}) custom-call(s32[2,32]{1,0:T(2,128)} %source_hbm.3, s32[2]{0:T(128)} %count_hbm.3, s32[16]{0:T(128)} %owner_hbm.3, s32[2,256]{1,0:T(2,128)} %domains_hbm.1, f32[2,256,256]{2,1,0:T(8,128)} %block_ref.5), custom_call_target="tpu_custom_call" | custom-call | tf_op jit(solution)/shard_map/pallas_call | solution.py:475
  1.8 5.1 %collective-permute-start = (s32[8,128]{1,0:T(8,128)S(1)}, s32[8,128]{1,0:T(8,128)S(1)}, u32[]{:S(2)}, u32[]{:S(2)}) collective-permute-start(s32[8,128]{1,0:T(8,128)S(1)} %get-tuple-element.14.message_ref), channel_id=1, source_target_pairs={{0,12},{5,8},{8,5},{12,0},{1,9},{4,13},{9,1},{13,4},{2,14},{7,10},... | collective-permute-start | bytes 12296 | tf_op jit(solution)/shard_map/ppermute | solution.py:529
  6.9 0.0 collective-permute-start.2
  6.9 1.6 %collective-permute-done.asked_ref = s32[8,128]{1,0:T(8,128)S(1)} collective-permute-done((s32[8,128]{1,0:T(8,128)S(1)}, s32[8,128]{1,0:T(8,128)S(1)}, u32[]{:S(2)}, u32[]{:S(2)}) %collective-permute-start) | collective-permute-done | bytes 4128 | tf_op jit(solution)/shard_map/ppermute | solution.py:529
  8.5 0.0 copy-done
  8.5 0.0 copy-start.1
  8.6 3.9 %collective-permute-start.1 = (f32[256,256]{1,0:T(8,128)S(1)}, f32[256,256]{1,0:T(8,128)S(1)}, u32[]{:S(2)}, u32[]{:S(2)}) collective-permute-start(f32[256,256]{1,0:T(8,128)S(1)} %shard_map.132), channel_id=1, source_target_pairs={{0,12},{5,8},{8,5},{12,0},{1,9},{4,13},{9,1},{13,4},{2,14},{7,10},... | collective-permute-start | bytes 786440 | tf_op jit(solution)/shard_map/ppermute | solution.py:533
  12.5 2.1 %shard_map.133 = (f32[2,8,256]{2,1,0:T(8,128)S(1)}, f32[8,256]{1,0:T(8,128)S(1)}, f32[768,128]{1,0:T(8,128)S(1)}) custom-call(f32[3,24000]{1,0:T(4,128)} %positions_hbm.1, f32[24000]{0:T(1024)} %energy_hbm.1, s32[8,128]{1,0:T(8,128)S(1)} %get-tuple-element.14.message_ref, s32[8,128]{1,0:T(8,128)S(1)} %collective-permute-done.asked_ref), custom_call_target="tpu_custom_call" | custom-call | flops 1000000000 | bytes 1000000 | tf_op jit(solution)/shard_map/pallas_call | solution.py:475
  14.6 0.0 copy-done.1
  14.6 3.4 %shard_map.134 = (f32[2,256,256]{2,1,0:T(8,128)S(1)}, f32[2,2,8,128]{3,2,1,0:T(8,128)S(1)}, f32[2,256,256]{2,1,0:T(8,128)S(1)}, f32[2,3,256,128]{3,2,1,0:T(8,128...) custom-call(f32[2,256,256]{2,1,0:T(8,128)S(1)} %copy-done, f32[2,256,256]{2,1,0:T(8,128)S(1)} %copy-done.1, ...), custom_call_target="tpu_custom_call" | custom-call | flops 20000000000 | bytes 40000000 | tf_op jit(solution)/shard_map/pallas_call | solution.py:475
  17.9 0.0 collective-permute-done.2.near_ref
  17.9 1.2 %shard_map.135.share_ref = f32[2,256,256]{2,1,0:T(8,128)S(1)} custom-call(f32[264,256]{1,0:T(8,128)S(1)} %collective-permute-done.2.near_ref, s32[8,128]{1,0:T(8,128)S(1)} %get-tuple-element.21.wanted_ref, f32[768,128]{1,0:T(8,128)S(1)} %get-tuple-element.22.table_ref, f32[2,3,256,128]{3,2,1,0:T(8,128)S(1)} %get-tuple-element.23.spread_ref, ...), custom_call_target="tpu_custom_call" | custom-call | flops 1000000000 | bytes 1000000 | tf_op jit(solution)/shard_map/pallas_call | solution.py:475
  19.1 0.6 %collective-permute-done.1.far_ref = f32[256,256]{1,0:T(8,128)S(1)} collective-permute-done((f32[256,256]{1,0:T(8,128)S(1)}, f32[256,256]{1,0:T(8,128)S(1)}, u32[]{:S(2)}, u32[]{:S(2)}) %collective-permute-start.1) | collective-permute-done | bytes 262176 | tf_op jit(solution)/shard_map/ppermute | solution.py:533
  19.8 0.7 %shard_map.136.share_ref = f32[2,256,256]{2,1,0:T(8,128)S(1)} custom-call(f32[256,256]{1,0:T(8,128)S(1)} %collective-permute-done.1.far_ref, bf16[2,256,256]{2,1,0:T(8,128)(2,1)S(1)} %get-tuple-element.17.high_ref, bf16[2,256,256]{2,1,0:T(8,128)(2,1)S(1)} %get-tuple-element.18.low_ref, f32[2,2,8,128]{3,2,1,0:T(8,128)S(1)} %get-tuple-element.19.weight_ref, ...), custom_call_target="tpu_custom_call" | custom-call | flops 1000000000 | bytes 1000000 | tf_op jit(solution)/shard_map/pallas_call | solution.py:475
  20.4 0.9 %collective-permute-start.3 = (f32[2,256,256]{2,1,0:T(8,128)S(1)}, f32[2,256,256]{2,1,0:T(8,128)S(1)}, u32[]{:S(2)}, u32[]{:S(2)}) collective-permute-start(f32[2,256,256]{2,1,0:T(8,128)S(1)} %shard_map.136.share_ref), channel_id=1, source_target_pairs={{0,1},{1,0},{2,3},{3,2},{4,5},{5,4},{6,7},{7,6},{8,9},{9,8},{10,11... | collective-permute-start | bytes 1572872 | tf_op jit(solution)/shard_map/ppermute | solution.py:597
  21.3 1.5 %collective-permute-done.3.other_ref = f32[2,256,256]{2,1,0:T(8,128)S(1)} collective-permute-done((f32[2,256,256]{2,1,0:T(8,128)S(1)}, f32[2,256,256]{2,1,0:T(8,128)S(1)}, u32[]{:S(2)}, u32[]{:S(2)}) %collective-permute-start.3) | collective-permute-done | bytes 524320 | tf_op jit(solution)/shard_map/ppermute | solution.py:597
  22.9 1.0 %shard_map.137 = (f32[2,256,256]{2,1,0:T(8,128)}, f32[2,256,256]{2,1,0:T(8,128)}) custom-call(f32[2,256,256]{2,1,0:T(8,128)S(1)} %shard_map.136.share_ref, f32[2,256,256]{2,1,0:T(8,128)S(1)} %collective-permute-done.3.other_ref, f32[2,256,256]{2,1,0:T(8,128)S(1)} %copy-done, f32[2,256,256]{2,1,0:T(8,128)S(1)} %get-tuple-element.25.inverse_ref), custom_call_target="tpu_custom_call" | custom-call | flops 1000000000 | bytes 1000000 | tf_op jit(solution)/shard_map/pallas_call | solution.py:475
  (1 shorter events, 0.0 us)
Async XLA Ops:
  0.6 7.9 %copy-start = (f32[2,256,256]{2,1,0:T(8,128)S(1)}, f32[2,256,256]{2,1,0:T(8,128)}, u32[]{:S(2)}) copy-start(f32[2,256,256]{2,1,0:T(8,128)} %block_ref.5) | copy-start | bytes 1572868
  1.8 6.7 %collective-permute-start = (s32[8,128]{1,0:T(8,128)S(1)}, s32[8,128]{1,0:T(8,128)S(1)}, u32[]{:S(2)}, u32[]{:S(2)}) collective-permute-start(s32[8,128]{1,0:T(8,128)S(1)} %get-tuple-element.14.message_ref), channel_id=1, source_target_pairs={{0,12},{5,8},{8,5},{12,0},{1,9},{4,13},{9,1},{13,4},{2,14},{7,10},... | collective-permute-start | bytes 12296 | tf_op jit(solution)/shard_map/ppermute | solution.py:529
  6.9 11.1 %collective-permute-start.2 = (f32[264,256]{1,0:T(8,128)S(1)}, f32[264,256]{1,0:T(8,128)S(1)}, u32[]{:S(2)}, u32[]{:S(2)}) collective-permute-start(f32[264,256]{1,0:T(8,128)S(1)} %get-tuple-element.20), channel_id=1, source_target_pairs={{0,4},{1,5},{4,0},{5,1},{8,12},{9,13},{12,8},{13,9},{2,6},{3,7},{6... | collective-permute-start | bytes 811016 | tf_op jit(solution)/shard_map/ppermute | solution.py:530
  8.5 6.0 %copy-start.1 = (f32[2,256,256]{2,1,0:T(8,128)S(1)}, f32[2,256,256]{2,1,0:T(8,128)}, u32[]{:S(2)}) copy-start(f32[2,256,256]{2,1,0:T(8,128)} %integrals_ref.1) | copy-start | bytes 1572868
  8.6 11.2 %collective-permute-start.1 = (f32[256,256]{1,0:T(8,128)S(1)}, f32[256,256]{1,0:T(8,128)S(1)}, u32[]{:S(2)}, u32[]{:S(2)}) collective-permute-start(f32[256,256]{1,0:T(8,128)S(1)} %shard_map.132), channel_id=1, source_target_pairs={{0,12},{5,8},{8,5},{12,0},{1,9},{4,13},{9,1},{13,4},{2,14},{7,10},... | collective-permute-start | bytes 786440 | tf_op jit(solution)/shard_map/ppermute | solution.py:533
  20.4 2.4 %collective-permute-start.3 = (f32[2,256,256]{2,1,0:T(8,128)S(1)}, f32[2,256,256]{2,1,0:T(8,128)S(1)}, u32[]{:S(2)}, u32[]{:S(2)}) collective-permute-start(f32[2,256,256]{2,1,0:T(8,128)S(1)} %shard_map.136.share_ref), channel_id=1, source_target_pairs={{0,1},{1,0},{2,3},{3,2},{4,5},{5,4},{6,7},{7,6},{8,9},{9,8},{10,11... | collective-permute-start | bytes 1572872 | tf_op jit(solution)/shard_map/ppermute | solution.py:597
